TPU v7x, 32 devices: a whole 2x2x4 slice. The times are simulated.
32 devices in a mesh: run: 2 (over y), tile: 4 (over z), site: 2 (over x), freq: 2 (over core).
Axes of the slice: x: 2, y: 2, z: 4, core: 2. Of those that a mesh axis runs over, the one named last changes fastest.
Arguments:
- jacobian: bfloat16 [256, 16, 8, 8, 128], P(('run', 'tile', 'site'), None, 'freq'), parts along dimension 0, may hold values from -6 to 6
- footprint: int32 [256, 16], P(('run', 'tile', 'site')), parts along dimension 0, may hold values from 0 to 4095, as said below
- home: int32 [8192], P('run'), parts along dimension 0, may hold values from 0 to 4095, as said below
- residual: float32 [256, 8, 8], P(('run', 'tile', 'site'), 'freq'), parts along dimension 0, may hold values from -6 to 6
- weights: float32 [256], P(('run', 'tile', 'site')), parts along dimension 0, may hold values from 0.2 to 2
- damping: float32 [8192, 128], P(('run', 'tile', 'site')), parts along dimension 0, may hold values from 2 to 50
- step_lengths: float32 [8], replicated, may hold values from 0.2 to 1.2
Outputs:
- model_step: float32 [8192, 128], P(('run', 'tile', 'site')), parts along dimension 0
- change: float32 [256, 8, 8], P(('run', 'tile', 'site'), 'freq'), parts along dimension 0
- curve: float32 [16, 8], P(('run', 'freq')), parts along dimension 0
There are 2 independent parts, one for each index of `run`. A program takes and returns all parts, laid end to end along the dimension named above; an argument that names none is the same for every part. Nothing has to cross between parts.
Inputs may be any that keep to these rules, and one draw needn't show every extreme that they name: home is a permutation of 0 to 4095. `footprint`: of the 256 entries of each aligned block of 16 sites, at most 64 have home[block] // 512 equal to any one value; one value receives exactly 64 entries from every such block.
All inputs are finite; a program needn't handle non-finite values.
Results may differ from a plain program's by a relative error of at most 0.0029.
Values may be sent and summed in bfloat16 or wider, within the bound.
A program may use at most 64 MiB of HBM per device.

v0:
```python
import jax
import jax.numpy as jnp
from jax import lax
from jax.sharding import PartitionSpec as P


def shards(jacobian, footprint, home, residual, weights, damping, step_lengths):
    site_count, foot_count, freq_local, comps, width = jacobian.shape
    blocks_dev = damping.shape[0]
    tiles = lax.axis_size("tile")
    groups = lax.axis_size("site")
    owner_count = tiles * groups
    entries = site_count * foot_count
    capacity = 2 * entries // owner_count
    weighted = (weights[:, None, None] * residual).astype(jnp.bfloat16)
    grad_terms = jnp.einsum(
        "skfcb,sfc->skb", jacobian, weighted, preferred_element_type=jnp.float32
    )
    curve_terms = weights[:, None, None] * jnp.sum(
        jnp.square(jacobian.astype(jnp.float32)), axis=(2, 3)
    )
    terms = jnp.concatenate([grad_terms, curve_terms], axis=-1).reshape(entries, 2 * width)
    position = home[footprint.reshape(-1)]
    dest_rank = position // blocks_dev
    local_slot = position % blocks_dev
    member = (dest_rank[:, None] == jnp.arange(owner_count, dtype=jnp.int32)[None, :]).astype(
        jnp.int32
    )
    earlier = jnp.cumsum(member, axis=0) - member
    order_in = jnp.sum(earlier * member, axis=1)
    bucket = dest_rank * capacity + order_in
    outgoing = jnp.zeros((owner_count * capacity, 2 * width), jnp.float32).at[bucket].set(terms)
    out_slots = (
        jnp.full((owner_count * capacity,), blocks_dev, jnp.int32).at[bucket].set(local_slot)
    )
    received, in_slots = (
        lax.all_to_all(
            outgoing.reshape(owner_count, capacity, 2 * width),
            ("tile", "site"),
            split_axis=0,
            concat_axis=0,
            tiled=True,
        ),
        lax.all_to_all(
            out_slots.reshape(owner_count, capacity),
            ("tile", "site"),
            split_axis=0,
            concat_axis=0,
            tiled=True,
        ),
    )
    flat_slots = in_slots.reshape(-1)
    totals = jax.ops.segment_sum(
        received.reshape(-1, 2 * width), flat_slots, num_segments=blocks_dev + 1
    )[:blocks_dev]
    totals = lax.psum(totals, "freq")
    model_step = totals[:, :width] / (totals[:, width:] + damping)
    step_low = jnp.concatenate(
        [model_step.astype(jnp.bfloat16), jnp.zeros((1, width), jnp.bfloat16)], axis=0
    )
    reply = step_low[flat_slots]
    returned = lax.all_to_all(
        reply.reshape(owner_count, capacity, width),
        ("tile", "site"),
        split_axis=0,
        concat_axis=0,
        tiled=True,
    )
    entry_rows = returned.reshape(owner_count * capacity, width)[bucket]
    entry_step = entry_rows.reshape(site_count, foot_count, width)
    change = jnp.einsum("skfcb,skb->sfc", jacobian, entry_step, preferred_element_type=jnp.float32)
    scale_total = site_count * owner_count * comps
    gap = residual[:, :, :, None] - step_lengths[None, None, None, :] * change[:, :, :, None]
    partial_sum = jnp.einsum("s,sfca->fa", weights, gap * gap)
    curve = lax.psum(partial_sum, ("tile", "site")) / scale_total
    return (model_step, change, curve)


def solution(mesh):
    placed = (
        P(("run", "tile", "site"), None, "freq", None, None),
        P(("run", "tile", "site"), None),
        P("run"),
        P(("run", "tile", "site"), "freq", None),
        P(("run", "tile", "site")),
        P(("run", "tile", "site"), None),
        P(),
    )
    return jax.shard_map(
        shards,
        mesh=mesh,
        in_specs=placed,
        out_specs=(
            P(("run", "tile", "site"), None),
            P(("run", "tile", "site"), "freq", None),
            P(("run", "freq"), None),
        ),
        check_vma=False,
    )
```

profile of v0, /device:TPU:0, one launch (start us, length us, event | category | flops | bytes accessed | tf_op | source)
XLA Modules:
  0.0 117.0 jit_solution(13052791357690887810)
XLA Ops:
  7.2 0.0 copy-start
  7.2 0.0 copy-start.1
  7.2 0.0 copy-start.5
  7.2 0.0 copy-start.4
  7.2 0.9 reshape.181
  8.2 0.0 copy-done
  8.2 1.7 %gather_fusion = s32[256]{0:T(256)S(1)} fusion(s32[4096]{0:T(1024)S(1)} %copy-done, s32[1024]{0:T(1024)S(1)} %pad_clamp_fusion.2), kind=kCustom, calls=%fused_computation | custom fusion | bytes 3072 | tf_op jit(solution)/shard_map/gather | solution.py:23
  9.9 0.6 reduce-window.6
  10.5 0.2 slice_reduce_fusion
  10.8 0.1 fusion.10
  10.9 1.4 %scatter_custom_fusion = s32[512]{0:T(512)S(1)} fusion(s32[256]{0:T(256)S(1)} %bitcast.64, s32[256]{0:T(256)S(1)} %get-tuple-element.5, s32[]{:T(128)} %constant.41.clone.1), kind=kCustom, calls=%fused_computation.49 | custom fusion | bytes 2052 | tf_op jit(solution)/shard_map/scatter | solution.py:34
  12.3 0.7 all_to_all.12
  13.0 7.3 %all-to-all-start = ((s32[8,1,64]{2,1,0:T(1,128)}), s32[8,1,64]{2,1,0:T(1,128)S(1)}, u32[]{:S(2)}, u32[]{:S(2)}) async-start(s32[8,1,64]{2,1,0:T(1,128)} %all_to_all.12), calls=%async_computation | async-start | bytes 8192 | tf_op jit(solution)/shard_map/all_to_all | solution.py:44
  20.2 2.3 %multiply_reduce_fusion = f32[16,16,128]{2,1,0:T(8,128)S(1)} fusion(bf16[16,16,4,8,128]{4,3,2,1,0:T(8,128)(2,1)} %param.7), kind=kLoop, calls=%fused_computation.6 | loop fusion | flops 3112960 | bytes 2228224 | tf_op jit(solution)/shard_map/reduce_sum | solution.py:19
  22.6 0.0 copy-done.5
  22.6 0.1 broadcast_multiply_fusion
  22.7 0.0 copy-done.4
  22.7 0.1 copy.14
  22.8 0.0 copy-done.1
  22.8 0.6 fusion.22
  23.4 0.0 copy-start.2
  23.4 2.2 %scatter_custom_fusion.1 = f32[512,256]{1,0:T(8,128)} fusion(s32[256]{0:T(256)S(1)} %bitcast.65, f32[256,256]{1,0:T(8,128)S(1)} %bitcast.56, f32[]{:T(128)} %constant.40.clone.1), kind=kCustom, calls=%fused_computation.14 | custom fusion | bytes 524292 | tf_op jit(solution)/shard_map/scatter | solution.py:32
  25.6 1.0 all-to-all-done
  26.6 5.0 %all-to-all-start.1 = ((f32[8,64,256]{2,1,0:T(8,128)}), f32[8,64,256]{2,1,0:T(8,128)S(1)}, u32[]{:S(2)}, u32[]{:S(2)}) async-start(f32[8,64,256]{2,1,0:T(8,128)} %bitcast.11), calls=%async_computation.1 | async-start | bytes 1048576 | tf_op jit(solution)/shard_map/all_to_all | solution.py:37
  31.6 0.0 all-reduce.3.cloned.1.call-start
  31.7 0.5 broadcast.204
  32.2 0.7 reduce.7
  32.8 0.1 reshape.231
  32.9 12.7 %all-to-all-done.1 = f32[8,64,256]{2,1,0:T(8,128)S(1)} async-done(((f32[8,64,256]{2,1,0:T(8,128)}), f32[8,64,256]{2,1,0:T(8,128)S(1)}, u32[]{:S(2)}, u32[]{:S(2)}) %all-to-all-start.1) | async-done | bytes 524320 | tf_op jit(solution)/shard_map/all_to_all | solution.py:37
  45.6 3.7 %scatter_custom_fusion.2 = f32[513,256]{1,0:T(8,128)S(1)} fusion(s32[512]{0:T(512)S(1)} %reshape.231, f32[512,256]{1,0:T(8,128)S(1)} %bitcast.54, f32[]{:T(128)} %constant.40.clone.1), kind=kCustom, calls=%fused_computation.9 | custom fusion | flops 131072 | bytes 525316 | tf_op jit(solution)/shard_map/scatter-add | solution.py:53
  49.3 0.8 slice.27
  50.1 0.0 all-reduce.3.cloned.1.call-update
  50.1 0.1 broadcast_in_dim_reshape.3
  50.2 17.9 %all-reduce.3.cloned.1.call-done = f32[512,256]{1,0:T(8,128)} async-done(((f32[512,256]{1,0:T(8,128)}), f32[512,256]{1,0:T(8,128)}) %all-reduce.3.cloned.1.call-update) | async-done | bytes 524304 | tf_op jit(solution)/shard_map/psum | solution.py:56
  68.1 0.0 copy-done.2
  68.1 1.8 %fusion.17 = (bf16[512,128]{1,0:T(8,128)(2,1)S(1)}, f32[512,128]{1,0:T(8,128)}) fusion(f32[512,128]{1,0:T(8,128)S(1)} %copy-done.2, f32[512,256]{1,0:T(8,128)} %all-reduce.3.cloned.1.call-done), kind=kLoop, calls=%fused_computation.55 | loop fusion | flops 196608 | bytes 1179648 | tf_op jit(solution)/shard_map/convert_element_type | solution.py:59
  69.9 1.9 %gather_fusion.1 = bf16[512,128]{1,0:T(8,128)(2,1)} fusion(bf16[513,128]{1,0:T(8,128)(2,1)S(1)} %concatenate.7, s32[1024]{0:T(1024)S(1)} %pad_clamp_fusion.1), kind=kCustom, calls=%fused_computation.1 | custom fusion | bytes 264192 | tf_op jit(solution)/shard_map/gather | solution.py:61
  71.8 5.8 %all-to-all-start.2 = ((bf16[8,64,128]{2,1,0:T(8,128)(2,1)}), bf16[8,64,128]{2,1,0:T(8,128)(2,1)S(1)}, u32[]{:S(2)}, u32[]{:S(2)}) async-start(bf16[8,64,128]{2,1,0:T(8,128)(2,1)} %bitcast.14), calls=%async_computation.2 | async-start | bytes 262144 | tf_op jit(solution)/shard_map/all_to_all | solution.py:62
  77.6 7.4 %all-to-all-done.2 = bf16[8,64,128]{2,1,0:T(8,128)(2,1)S(1)} async-done(((bf16[8,64,128]{2,1,0:T(8,128)(2,1)}), bf16[8,64,128]{2,1,0:T(8,128)(2,1)S(1)}, u32[]{:S(2)}, u32[]{:S(2)}) %all-to-all-start.2) | async-done | bytes 131104 | tf_op jit(solution)/shard_map/all_to_all | solution.py:62
  85.1 0.0 copy-start.6
  85.1 0.9 gather_fusion.2
  85.9 4.7 %fusion = f32[16,1,4,8,1]{3,1,4,2,0:T(1,128)S(1)} fusion(bf16[16,16,4,8,128]{4,3,2,1,0:T(8,128)(2,1)S(1)} %copy-done.1, bf16[16,16,128,1,1]{2,1,0,3,4:T(8,128)(2,1)S(1)} %bitcast.57), kind=kOutput, calls=%fused_computation.7 | convolution fusion | flops 2097152 | bytes 2164736 | tf_op jit(solution)/shard_map/skfcb,skb->sfc/dot_general | solution.py:71
  90.6 0.1 copy.18
  90.7 0.0 copy-start.3
  90.7 0.0 copy-done.6
  90.7 0.1 multiply_reduce_fusion.1
  90.8 0.1 fusion.19
  91.0 18.6 %psum.15 = f32[4,8]{1,0:T(4,128)S(1)} all-reduce(f32[4,8]{1,0:T(4,128)S(1)} %bitcast.63), channel_id=1, replica_groups=mesh['run'=2,'tile'=4,'site'=2,'freq'=2] {'tile','site'}, use_global_device_ids=true, to_apply=%region_9.10 | all-reduce | flops 32 | bytes 256 | tf_op jit(solution)/shard_map/psum | solution.py:75
  109.5 0.6 broadcast_multiply_fusion.1
  110.1 0.0 copy-done.3
  (14 shorter events, 0.2 us)
Async XLA Ops:
  7.2 1.0 copy-start
  7.2 15.6 %copy-start.1 = (bf16[16,16,4,8,128]{4,3,2,1,0:T(8,128)(2,1)S(1)}, bf16[16,16,4,8,128]{4,3,2,1,0:T(8,128)(2,1)}, u32[]{:S(2)}) copy-start(bf16[16,16,4,8,128]{4,3,2,1,0:T(8,128)(2,1)} %param.7) | copy-start | bytes 6291460
  7.2 15.4 %copy-start.5 = (f32[16]{0:T(128)S(1)}, f32[16]{0:T(128)}, u32[]{:S(2)}) copy-start(f32[16]{0:T(128)} %param.11) | copy-start | bytes 196
  7.2 15.5 %copy-start.4 = (f32[16,4,8]{0,2,1:T(8,128)S(1)}, f32[16,4,8]{0,2,1:T(8,128)}, u32[]{:S(2)}) copy-start(f32[16,4,8]{0,2,1:T(8,128)} %param.10) | copy-start | bytes 6148
  13.0 13.6 %all-to-all-start = ((s32[8,1,64]{2,1,0:T(1,128)}), s32[8,1,64]{2,1,0:T(1,128)S(1)}, u32[]{:S(2)}, u32[]{:S(2)}) async-start(s32[8,1,64]{2,1,0:T(1,128)} %all_to_all.12), calls=%async_computation | async-start | bytes 8192 | tf_op jit(solution)/shard_map/all_to_all | solution.py:44
  23.4 44.7 %copy-start.2 = (f32[512,128]{1,0:T(8,128)S(1)}, f32[512,128]{1,0:T(8,128)}, u32[]{:S(2)}) copy-start(f32[512,128]{1,0:T(8,128)} %param.12) | copy-start | bytes 786436
  26.6 19.0 %all-to-all-start.1 = ((f32[8,64,256]{2,1,0:T(8,128)}), f32[8,64,256]{2,1,0:T(8,128)S(1)}, u32[]{:S(2)}, u32[]{:S(2)}) async-start(f32[8,64,256]{2,1,0:T(8,128)} %bitcast.11), calls=%async_computation.1 | async-start | bytes 1048576 | tf_op jit(solution)/shard_map/all_to_all | solution.py:37
  31.6 36.5 %all-reduce.3.cloned.1.call-start = ((), (), s32[]{:S(2)}) async-start(), calls=%async_computation.3 | async-start | bytes 1048576 | tf_op jit(solution)/shard_map/psum | solution.py:56
  71.8 13.2 %all-to-all-start.2 = ((bf16[8,64,128]{2,1,0:T(8,128)(2,1)}), bf16[8,64,128]{2,1,0:T(8,128)(2,1)S(1)}, u32[]{:S(2)}, u32[]{:S(2)}) async-start(bf16[8,64,128]{2,1,0:T(8,128)(2,1)} %bitcast.14), calls=%async_computation.2 | async-start | bytes 262144 | tf_op jit(solution)/shard_map/all_to_all | solution.py:62
  85.1 5.6 %copy-start.6 = (f32[8]{0:T(128)S(1)}, f32[8]{0:T(128)}, u32[]{:S(2)}) copy-start(f32[8]{0:T(128)} %param.13) | copy-start | bytes 100
  90.7 19.4 %copy-start.3 = (f32[16,1,4,8,1]{0,3,2,1,4:T(8,128)}, f32[16,1,4,8,1]{0,3,2,1,4:T(8,128)S(1)}, u32[]{:S(2)}) copy-start(f32[16,1,4,8,1]{0,3,2,1,4:T(8,128)S(1)} %copy.18) | copy-start | bytes 6148
Sparse Core Ops, SparseCore 0:
  50.3 17.8 all-reduce.2
where the time goes:
time: 117 us
  waiting for transfers between devices  39 us (33%)
  blocking collectives  18.6 us (16%)
  starting transfers between devices  18.1 us (15%)
  between operations  14.2 us (12%)
  local copies, waits for them, and re-layouts  11.6 us (10%)
  other arithmetic  10.1 us (9%)
  matrix products  5.41 us (5%)
    psum x1, blocking collectives, shards(): curve = lax.psum(partial_sum, ('tile', 'site')) / scale_total  18.6 us
    psum x1, waiting for transfers between devices, shards(): totals = lax.psum(totals, 'freq')  17.9 us
    all_to_all x1, waiting for transfers between devices, shards(): lax.all_to_all(outgoing.reshape(owner_count, capacity, 2 * width), ('tile...  12.7 us
    all_to_all x1, waiting for transfers between devices, shards(): lax.all_to_all(reply.reshape(owner_count, capacity, width), ('tile', 'sit...  7.43 us
    all_to_all x1, starting transfers between devices, shards(): lax.all_to_all(out_slots.reshape(owner_count, capacity), ('tile', 'site')...  7.25 us
    all_to_all x1, starting transfers between devices, shards(): lax.all_to_all(reply.reshape(owner_count, capacity, width), ('tile', 'sit...  5.78 us
    all_to_all x1, starting transfers between devices, shards(): lax.all_to_all(outgoing.reshape(owner_count, capacity, 2 * width), ('tile...  5 us
    dot_general x1, matrix products, shards(): jnp.einsum('skfcb,skb->sfc', jacobian, entry_step, preferred_element_type...  4.69 us
  transfers between devices with their start and end apart: 4, of which 4 were waited for; matrix products, arithmetic and copies ran while one was open for 6% of the time, Pallas kernels for 0%

commit v1 on v0

--- a/solution.py
+++ b/solution.py
@@ -72,7 +72,7 @@
     scale_total = site_count * owner_count * comps
     gap = residual[:, :, :, None] - step_lengths[None, None, None, :] * change[:, :, :, None]
     partial_sum = jnp.einsum("s,sfca->fa", weights, gap * gap)
-    curve = lax.psum(partial_sum, ("tile", "site")) / scale_total
+    curve = lax.psum(lax.psum(partial_sum, "site"), "tile") / scale_total
     return (model_step, change, curve)
 
 

time: 117 us -> 113 us (0.966)
  blocking collectives: 18.6 us -> 13.8 us
    psum x1 -> x2, blocking collectives: 18.6 us -> 13.8 us  [shards(): curve = lax.psum(lax.psum(partial_sum, 'site'), 'tile') / scale_total]
where the time goes in v1:
time: 113 us; the launch traced here: 112 us
  waiting for transfers between devices  39 us (35%)
  starting transfers between devices  18.1 us (16%)
  between operations  14.2 us (13%)
  blocking collectives  13.8 us (12%)
  local copies, waits for them, and re-layouts  11.6 us (10%)
  other arithmetic  10.1 us (9%)
  matrix products  5.41 us (5%)
    psum x1, waiting for transfers between devices, shards(): totals = lax.psum(totals, 'freq')  17.9 us
    psum x2, blocking collectives, shards(): curve = lax.psum(lax.psum(partial_sum, 'site'), 'tile') / scale_total  13.8 us
    all_to_all x1, waiting for transfers between devices, shards(): lax.all_to_all(outgoing.reshape(owner_count, capacity, 2 * width), ('tile...  12.7 us
    all_to_all x1, waiting for transfers between devices, shards(): lax.all_to_all(reply.reshape(owner_count, capacity, width), ('tile', 'sit...  7.43 us
    all_to_all x1, starting transfers between devices, shards(): lax.all_to_all(out_slots.reshape(owner_count, capacity), ('tile', 'site')...  7.25 us
    all_to_all x1, starting transfers between devices, shards(): lax.all_to_all(reply.reshape(owner_count, capacity, width), ('tile', 'sit...  5.78 us
    all_to_all x1, starting transfers between devices, shards(): lax.all_to_all(outgoing.reshape(owner_count, capacity, 2 * width), ('tile...  5 us
    dot_general x1, matrix products, shards(): jnp.einsum('skfcb,skb->sfc', jacobian, entry_step, preferred_element_type...  4.69 us
  transfers between devices with their start and end apart: 4, of which 4 were waited for; matrix products, arithmetic and copies ran while one was open for 6% of the time, Pallas kernels for 0%

profile of v1, /device:TPU:0, one launch (start us, length us, event | category | flops | bytes accessed | tf_op | source)
XLA Modules:
  0.0 112.2 jit_solution(8782822702730653970)
XLA Ops:
  7.2 0.0 copy-start
  7.2 0.0 copy-start.1
  7.2 0.0 copy-start.5
  7.2 0.0 copy-start.4
  7.2 0.9 reshape.181
  8.2 0.0 copy-done
  8.2 1.7 %gather_fusion = s32[256]{0:T(256)S(1)} fusion(s32[4096]{0:T(1024)S(1)} %copy-done, s32[1024]{0:T(1024)S(1)} %pad_clamp_fusion.2), kind=kCustom, calls=%fused_computation | custom fusion | bytes 3072 | tf_op jit(solution)/shard_map/gather | solution.py:23
  9.9 0.6 reduce-window.6
  10.5 0.2 slice_reduce_fusion
  10.8 0.1 fusion.10
  10.9 1.4 %scatter_custom_fusion = s32[512]{0:T(512)S(1)} fusion(s32[256]{0:T(256)S(1)} %bitcast.64, s32[256]{0:T(256)S(1)} %get-tuple-element.5, s32[]{:T(128)} %constant.41.clone.1), kind=kCustom, calls=%fused_computation.49 | custom fusion | bytes 2052 | tf_op jit(solution)/shard_map/scatter | solution.py:34
  12.3 0.7 all_to_all.12
  13.0 7.3 %all-to-all-start = ((s32[8,1,64]{2,1,0:T(1,128)}), s32[8,1,64]{2,1,0:T(1,128)S(1)}, u32[]{:S(2)}, u32[]{:S(2)}) async-start(s32[8,1,64]{2,1,0:T(1,128)} %all_to_all.12), calls=%async_computation | async-start | bytes 8192 | tf_op jit(solution)/shard_map/all_to_all | solution.py:44
  20.2 2.3 %multiply_reduce_fusion = f32[16,16,128]{2,1,0:T(8,128)S(1)} fusion(bf16[16,16,4,8,128]{4,3,2,1,0:T(8,128)(2,1)} %param.7), kind=kLoop, calls=%fused_computation.6 | loop fusion | flops 3112960 | bytes 2228224 | tf_op jit(solution)/shard_map/reduce_sum | solution.py:19
  22.6 0.0 copy-done.5
  22.6 0.1 broadcast_multiply_fusion
  22.7 0.0 copy-done.4
  22.7 0.1 copy.14
  22.8 0.0 copy-done.1
  22.8 0.6 fusion.22
  23.4 0.0 copy-start.2
  23.4 2.2 %scatter_custom_fusion.1 = f32[512,256]{1,0:T(8,128)} fusion(s32[256]{0:T(256)S(1)} %bitcast.65, f32[256,256]{1,0:T(8,128)S(1)} %bitcast.56, f32[]{:T(128)} %constant.40.clone.1), kind=kCustom, calls=%fused_computation.14 | custom fusion | bytes 524292 | tf_op jit(solution)/shard_map/scatter | solution.py:32
  25.6 1.0 all-to-all-done
  26.6 5.0 %all-to-all-start.1 = ((f32[8,64,256]{2,1,0:T(8,128)}), f32[8,64,256]{2,1,0:T(8,128)S(1)}, u32[]{:S(2)}, u32[]{:S(2)}) async-start(f32[8,64,256]{2,1,0:T(8,128)} %bitcast.11), calls=%async_computation.1 | async-start | bytes 1048576 | tf_op jit(solution)/shard_map/all_to_all | solution.py:37
  31.6 0.0 all-reduce.3.cloned.1.call-start
  31.7 0.5 broadcast.204
  32.2 0.7 reduce.7
  32.8 0.1 reshape.231
  32.9 12.7 %all-to-all-done.1 = f32[8,64,256]{2,1,0:T(8,128)S(1)} async-done(((f32[8,64,256]{2,1,0:T(8,128)}), f32[8,64,256]{2,1,0:T(8,128)S(1)}, u32[]{:S(2)}, u32[]{:S(2)}) %all-to-all-start.1) | async-done | bytes 524320 | tf_op jit(solution)/shard_map/all_to_all | solution.py:37
  45.6 3.7 %scatter_custom_fusion.2 = f32[513,256]{1,0:T(8,128)S(1)} fusion(s32[512]{0:T(512)S(1)} %reshape.231, f32[512,256]{1,0:T(8,128)S(1)} %bitcast.54, f32[]{:T(128)} %constant.40.clone.1), kind=kCustom, calls=%fused_computation.9 | custom fusion | flops 131072 | bytes 525316 | tf_op jit(solution)/shard_map/scatter-add | solution.py:53
  49.3 0.8 slice.27
  50.1 0.0 all-reduce.3.cloned.1.call-update
  50.1 0.1 broadcast_in_dim_reshape.3
  50.2 17.9 %all-reduce.3.cloned.1.call-done = f32[512,256]{1,0:T(8,128)} async-done(((f32[512,256]{1,0:T(8,128)}), f32[512,256]{1,0:T(8,128)}) %all-reduce.3.cloned.1.call-update) | async-done | bytes 524304 | tf_op jit(solution)/shard_map/psum | solution.py:56
  68.1 0.0 copy-done.2
  68.1 1.8 %fusion.17 = (bf16[512,128]{1,0:T(8,128)(2,1)S(1)}, f32[512,128]{1,0:T(8,128)}) fusion(f32[512,128]{1,0:T(8,128)S(1)} %copy-done.2, f32[512,256]{1,0:T(8,128)} %all-reduce.3.cloned.1.call-done), kind=kLoop, calls=%fused_computation.55 | loop fusion | flops 196608 | bytes 1179648 | tf_op jit(solution)/shard_map/convert_element_type | solution.py:59
  69.9 1.9 %gather_fusion.1 = bf16[512,128]{1,0:T(8,128)(2,1)} fusion(bf16[513,128]{1,0:T(8,128)(2,1)S(1)} %concatenate.7, s32[1024]{0:T(1024)S(1)} %pad_clamp_fusion.1), kind=kCustom, calls=%fused_computation.1 | custom fusion | bytes 264192 | tf_op jit(solution)/shard_map/gather | solution.py:61
  71.8 5.8 %all-to-all-start.2 = ((bf16[8,64,128]{2,1,0:T(8,128)(2,1)}), bf16[8,64,128]{2,1,0:T(8,128)(2,1)S(1)}, u32[]{:S(2)}, u32[]{:S(2)}) async-start(bf16[8,64,128]{2,1,0:T(8,128)(2,1)} %bitcast.14), calls=%async_computation.2 | async-start | bytes 262144 | tf_op jit(solution)/shard_map/all_to_all | solution.py:62
  77.6 7.4 %all-to-all-done.2 = bf16[8,64,128]{2,1,0:T(8,128)(2,1)S(1)} async-done(((bf16[8,64,128]{2,1,0:T(8,128)(2,1)}), bf16[8,64,128]{2,1,0:T(8,128)(2,1)S(1)}, u32[]{:S(2)}, u32[]{:S(2)}) %all-to-all-start.2) | async-done | bytes 131104 | tf_op jit(solution)/shard_map/all_to_all | solution.py:62
  85.1 0.0 copy-start.6
  85.1 0.9 gather_fusion.2
  85.9 4.7 %fusion = f32[16,1,4,8,1]{3,1,4,2,0:T(1,128)S(1)} fusion(bf16[16,16,4,8,128]{4,3,2,1,0:T(8,128)(2,1)S(1)} %copy-done.1, bf16[16,16,128,1,1]{2,1,0,3,4:T(8,128)(2,1)S(1)} %bitcast.57), kind=kOutput, calls=%fused_computation.7 | convolution fusion | flops 2097152 | bytes 2164736 | tf_op jit(solution)/shard_map/skfcb,skb->sfc/dot_general | solution.py:71
  90.6 0.1 copy.18
  90.7 0.0 copy-start.3
  90.7 0.0 copy-done.6
  90.7 0.1 multiply_reduce_fusion.1
  90.8 0.1 fusion.19
  91.0 4.9 %psum.22 = f32[4,8]{1,0:T(4,128)S(1)} all-reduce(f32[4,8]{1,0:T(4,128)S(1)} %bitcast.63), channel_id=1, replica_groups=mesh['run'=2,'tile'=4,'site'=2,'freq'=2] {'site'}, use_global_device_ids=true, to_apply=%region_9.10 | all-reduce | flops 32 | bytes 256 | tf_op jit(solution)/shard_map/psum | solution.py:75
  95.9 8.9 %psum.23 = f32[4,8]{1,0:T(4,128)S(1)} all-reduce(f32[4,8]{1,0:T(4,128)S(1)} %psum.22), channel_id=1, replica_groups=mesh['run'=2,'tile'=4,'site'=2,'freq'=2] {'tile'}, use_global_device_ids=true, to_apply=%region_10.11 | all-reduce | flops 32 | bytes 256 | tf_op jit(solution)/shard_map/psum | solution.py:75
  104.8 0.6 broadcast_multiply_fusion.1
  105.4 0.0 copy-done.3
  (14 shorter events, 0.2 us)
Async XLA Ops:
  7.2 1.0 copy-start
  7.2 15.6 %copy-start.1 = (bf16[16,16,4,8,128]{4,3,2,1,0:T(8,128)(2,1)S(1)}, bf16[16,16,4,8,128]{4,3,2,1,0:T(8,128)(2,1)}, u32[]{:S(2)}) copy-start(bf16[16,16,4,8,128]{4,3,2,1,0:T(8,128)(2,1)} %param.7) | copy-start | bytes 6291460
  7.2 15.4 %copy-start.5 = (f32[16]{0:T(128)S(1)}, f32[16]{0:T(128)}, u32[]{:S(2)}) copy-start(f32[16]{0:T(128)} %param.11) | copy-start | bytes 196
  7.2 15.5 %copy-start.4 = (f32[16,4,8]{0,2,1:T(8,128)S(1)}, f32[16,4,8]{0,2,1:T(8,128)}, u32[]{:S(2)}) copy-start(f32[16,4,8]{0,2,1:T(8,128)} %param.10) | copy-start | bytes 6148
  13.0 13.6 %all-to-all-start = ((s32[8,1,64]{2,1,0:T(1,128)}), s32[8,1,64]{2,1,0:T(1,128)S(1)}, u32[]{:S(2)}, u32[]{:S(2)}) async-start(s32[8,1,64]{2,1,0:T(1,128)} %all_to_all.12), calls=%async_computation | async-start | bytes 8192 | tf_op jit(solution)/shard_map/all_to_all | solution.py:44
  23.4 44.7 %copy-start.2 = (f32[512,128]{1,0:T(8,128)S(1)}, f32[512,128]{1,0:T(8,128)}, u32[]{:S(2)}) copy-start(f32[512,128]{1,0:T(8,128)} %param.12) | copy-start | bytes 786436
  26.6 19.0 %all-to-all-start.1 = ((f32[8,64,256]{2,1,0:T(8,128)}), f32[8,64,256]{2,1,0:T(8,128)S(1)}, u32[]{:S(2)}, u32[]{:S(2)}) async-start(f32[8,64,256]{2,1,0:T(8,128)} %bitcast.11), calls=%async_computation.1 | async-start | bytes 1048576 | tf_op jit(solution)/shard_map/all_to_all | solution.py:37
  31.6 36.5 %all-reduce.3.cloned.1.call-start = ((), (), s32[]{:S(2)}) async-start(), calls=%async_computation.3 | async-start | bytes 1048576 | tf_op jit(solution)/shard_map/psum | solution.py:56
  71.8 13.2 %all-to-all-start.2 = ((bf16[8,64,128]{2,1,0:T(8,128)(2,1)}), bf16[8,64,128]{2,1,0:T(8,128)(2,1)S(1)}, u32[]{:S(2)}, u32[]{:S(2)}) async-start(bf16[8,64,128]{2,1,0:T(8,128)(2,1)} %bitcast.14), calls=%async_computation.2 | async-start | bytes 262144 | tf_op jit(solution)/shard_map/all_to_all | solution.py:62
  85.1 5.6 %copy-start.6 = (f32[8]{0:T(128)S(1)}, f32[8]{0:T(128)}, u32[]{:S(2)}) copy-start(f32[8]{0:T(128)} %param.13) | copy-start | bytes 100
  90.7 14.7 %copy-start.3 = (f32[16,1,4,8,1]{0,3,2,1,4:T(8,128)}, f32[16,1,4,8,1]{0,3,2,1,4:T(8,128)S(1)}, u32[]{:S(2)}) copy-start(f32[16,1,4,8,1]{0,3,2,1,4:T(8,128)S(1)} %copy.18) | copy-start | bytes 6148
Sparse Core Ops, SparseCore 0:
  50.3 17.8 all-reduce.2
